TPU v7x, 32 devices: a whole 2x2x4 slice. The times are simulated.
32 devices in a mesh: row: 4 (over x, core), col: 8 (over z, y).
Axes of the slice: x: 2, y: 2, z: 4, core: 2. Of those that a mesh axis runs over, the one named last changes fastest.
Arguments:
- jac: bfloat16 [768, 16384], P(('row', 'col')), may hold values from -0.21875 to 0.21875
- owner_list: int32 [768, 1], replicated, may hold values from 0 to 7; in each aligned block of 24 rows (0 to 23, 24 to 47, ...) at most 6 rows name the same one
- block_id: int32 [768], replicated, may hold values from 0 to 7
- diag_weight: float32 [64], replicated, may hold values from 0.25 to 4
- corr_weight: float32 [64], replicated, may hold values from 0.1 to 1
Outputs:
- gn_matrix: float32 [16384, 16384], P('row', 'col')
Inputs may be any that keep to these rules, and one draw needn't show every extreme that they name: `owner_list`: among the 24 points of one mesh owner (aligned blocks of rows) no panel owner is named more than 6 times, and in some block one is named exactly 6 times.
All inputs are finite; a program needn't handle non-finite values.
Results may differ from a plain program's by a relative error of at most 0.0039.
Values may be sent and summed in bfloat16 or wider, within the bound.
A program may use at most 128 MiB of HBM per device.

v0:
```python
import jax
import jax.numpy as jnp
from jax import lax
from jax.sharding import PartitionSpec as P

BPC = 8


def from_root(value, axis, source):
    kept = jnp.where(lax.axis_index(axis) == source, value, 0).astype(value.dtype)
    return lax.psum(kept, axis)


def local(jac, owner_list, block_id, diag_weight, corr_weight):
    n_row = lax.axis_size("row")
    n_col = lax.axis_size("col")
    my_col = lax.axis_index("col")
    pt_dev = jac.shape[0]
    width = jac.shape[1]
    win = width // n_col
    points = owner_list.shape[0]
    nblocks = n_col * BPC
    cap_slots = max(2, (2 * pt_dev + n_col - 1) // n_col)
    per_src = n_row * cap_slots
    local_rows = lax.all_to_all(jac, "row", split_axis=1, concat_axis=0, tiled=True)
    target = owner_list[:, 0]
    group = target * BPC + block_id
    table_hit = group[:, None] == jnp.arange(nblocks, dtype=jnp.int32)[None, :]
    point_scale = jnp.sum(jnp.where(table_hit, diag_weight[None, :], 0.0), axis=1)
    owner_dest = target.reshape(points // pt_dev, pt_dev)
    earlier = jnp.arange(pt_dev)[None, :] < jnp.arange(pt_dev)[:, None]
    same_dest = owner_dest[:, :, None] == owner_dest[:, None, :]
    rank = jnp.sum((same_dest & earlier[None, :, :]).astype(jnp.int32), axis=2).reshape(points)
    pid_grid = (
        (
            jnp.arange(n_row, dtype=jnp.int32)[None, :, None] * n_col
            + jnp.arange(n_col, dtype=jnp.int32)[:, None, None]
        )
        * pt_dev
        + jnp.arange(pt_dev, dtype=jnp.int32)[None, None, :]
    ).reshape(n_col, n_row * pt_dev)
    pid_local = lax.dynamic_index_in_dim(pid_grid, my_col, 0, keepdims=False)
    src_row = jnp.arange(n_row * pt_dev, dtype=jnp.int32) // pt_dev
    slot_target = target[pid_local] * per_src + src_row * cap_slots + rank[pid_local]
    select = (jnp.arange(n_col * per_src, dtype=jnp.int32)[:, None] == slot_target[None, :]).astype(
        jnp.bfloat16
    )
    outgoing = jnp.dot(select, local_rows, preferred_element_type=jnp.float32).astype(jnp.bfloat16)
    incoming = lax.all_to_all(outgoing, "col", split_axis=0, concat_axis=0, tiled=True)
    every = jnp.arange(points, dtype=jnp.int32)
    src_col = every // pt_dev % n_col
    src_owner_row = every // pt_dev // n_col
    slot_index = src_col * per_src + src_owner_row * cap_slots + rank
    total_slots = n_col * per_src
    slot_place = jnp.where(target == my_col, slot_index, total_slots)
    slot_block = jnp.full((total_slots,), -1, jnp.int32).at[slot_place].set(block_id, mode="drop")
    member = (jnp.arange(BPC, dtype=jnp.int32)[:, None] == slot_block[None, :]).astype(jnp.bfloat16)
    own_sums = jnp.dot(member, incoming, preferred_element_type=jnp.float32).astype(jnp.bfloat16)
    panel = jnp.concatenate([local_rows, own_sums], axis=0)
    scales = jnp.concatenate(
        [point_scale[pid_grid], corr_weight.reshape(n_col, BPC)], axis=1
    ).reshape(-1)
    gathered = lax.all_gather(panel, "col", axis=0, tiled=True)
    per_row = n_col // n_row
    offset = my_col % per_row * win
    piece = lax.dynamic_slice_in_dim(gathered, offset, win, 1)
    window = from_root(piece, "row", my_col // per_row)
    scaled = (scales[:, None] * window.astype(jnp.float32)).astype(jnp.bfloat16)
    return lax.dot_general(
        gathered, scaled, (((0,), (0,)), ((), ())), preferred_element_type=jnp.float32
    )


def solution(mesh):
    in_specs = (P(("row", "col"), None), P(), P(), P(), P())
    out_specs = P("row", "col")
    return jax.shard_map(local, mesh=mesh, in_specs=in_specs, out_specs=out_specs, check_vma=False)
```

profile of v0, /device:TPU:7, one launch (start us, length us, event | category | flops | bytes accessed | tf_op | source)
XLA Modules:
  0.0 280.5 jit_solution(7768048429168767621)
XLA Ops:
  6.5 2.1 copy.15
  8.6 4.3 %all-to-all-start = ((bf16[24,4,4096]{2,0,1:T(8,128)(2,1)}), bf16[24,4,4096]{2,0,1:T(8,128)(2,1)S(1)}, u32[]{:S(2)}, u32[]{:S(2)}) async-start(bf16[24,4,4096]{2,0,1:T(8,128)(2,1)} %bitcast.17), calls=%async_computation | async-start | bytes 1572864 | tf_op jit(solution)/shard_map/all_to_all | solution.py:25
  12.9 0.1 add.187
  13.1 0.1 add.185
  13.2 0.7 reduce
  14.0 1.0 gather_fusion
  15.1 0.2 convert_reduce_fusion
  15.3 0.1 reshape.278
  15.4 1.0 gather_fusion.1
  16.4 6.3 %all-to-all-done = bf16[24,4,4096]{2,0,1:T(8,128)(2,1)S(1)} async-done(((bf16[24,4,4096]{2,0,1:T(8,128)(2,1)}), bf16[24,4,4096]{2,0,1:T(8,128)(2,1)S(1)}, u32[]{:S(2)}, u32[]{:S(2)}) %all-to-all-start) | async-done | bytes 786464 | tf_op jit(solution)/shard_map/all_to_all | solution.py:25
  22.7 1.7 convolution_convert_fusion
  24.4 5.8 %all-to-all-start.1 = ((bf16[8,24,4096]{2,1,0:T(8,128)(2,1)}), bf16[8,24,4096]{2,1,0:T(8,128)(2,1)S(1)}, u32[]{:S(2)}, u32[]{:S(2)}) async-start(bf16[8,24,4096]{2,1,0:T(8,128)(2,1)} %bitcast.22), calls=%async_computation.1 | async-start | bytes 3145728 | tf_op jit(solution)/shard_map/all_to_all | solution.py:49
  30.1 0.1 reshape.277
  30.3 3.4 %scatter_custom_fusion = s32[192]{0:T(256)S(1)} fusion(s32[768]{0:T(1024)S(1)} %fusion.4, s32[768]{0:T(1024)S(1)} %copy-done.1, s32[]{:T(128)} %constant.84.clone.1), kind=kCustom, calls=%fused_computation.52 | custom fusion | bytes 772 | tf_op jit(solution)/shard_map/scatter | solution.py:56
  33.7 32.6 %all-to-all-done.1 = bf16[8,24,4096]{2,1,0:T(8,128)(2,1)S(1)} async-done(((bf16[8,24,4096]{2,1,0:T(8,128)(2,1)}), bf16[8,24,4096]{2,1,0:T(8,128)(2,1)S(1)}, u32[]{:S(2)}, u32[]{:S(2)}) %all-to-all-start.1) | async-done | bytes 1572896 | tf_op jit(solution)/shard_map/all_to_all | solution.py:49
  66.3 0.3 convolution_convert_fusion.1
  66.6 1.0 pad_maximum_fusion
  67.7 104.2 %all-gather.2.cloned.1.call-done = bf16[832,4096]{1,0:T(8,128)(2,1)} async-done(((bf16[104,4096]{1,0:T(8,128)(2,1)}), bf16[832,4096]{1,0:T(8,128)(2,1)}) %all-gather.2.cloned.1.call-update) | async-done | bytes 6815760 | tf_op jit(solution)/shard_map/all_gather | solution.py:63
  171.9 4.7 %dynamic-slice_select_fusion = bf16[832,2048]{1,0:T(8,128)(2,1)} fusion(bf16[832,4096]{1,0:T(8,128)(2,1)} %all-gather.2.cloned.1.call-done, s32[]{:T(128)S(6)} %select_n.118, pred[]{:T(512)S(6)} %eq.83), kind=kLoop, calls=%fused_computation.8 | loop fusion | flops 1703936 | bytes 6815749 | tf_op jit(solution)/shard_map/jit(_where)/select_n | solution.py:10
  176.7 0.5 copy-done.2
  177.4 0.1 select_reduce_fusion
  177.5 3.2 %gather_fusion.2 = f32[768]{0:T(1024)S(1)} fusion(f32[768]{0:T(1024)S(1)} %select_reduce_fusion, s32[1024]{0:T(1024)S(1)} %pad_clamp_fusion), kind=kCustom, calls=%fused_computation.2 | custom fusion | bytes 9216 | tf_op jit(solution)/shard_map/gather | solution.py:61
  180.9 67.4 %all-reduce.2.cloned.1.call-done = bf16[832,2048]{1,0:T(8,128)(2,1)} async-done(((bf16[832,2048]{1,0:T(8,128)(2,1)}), bf16[832,2048]{1,0:T(8,128)(2,1)}) %all-reduce.2.cloned.1.call-update) | async-done | bytes 3407888 | tf_op jit(solution)/shard_map/psum | solution.py:11
  248.3 25.3 %fusion = f32[4096,2048]{1,0:T(8,128)} fusion(bf16[832,4096]{1,0:T(8,128)(2,1)} %all-gather.2.cloned.1.call-done, bf16[832,2048]{1,0:T(8,128)(2,1)} %all-reduce.2.cloned.1.call-done, f32[832]{0:T(1024)S(1)} %mul.95), kind=kOutput, calls=%fused_computation.7 | convolution fusion | flops 13963755520 | bytes 43781376 | tf_op jit(solution)/shard_map/dot_general | solution.py:69
  (33 shorter events, 1.0 us)
Async XLA Ops:
  8.6 14.1 %all-to-all-start = ((bf16[24,4,4096]{2,0,1:T(8,128)(2,1)}), bf16[24,4,4096]{2,0,1:T(8,128)(2,1)S(1)}, u32[]{:S(2)}, u32[]{:S(2)}) async-start(bf16[24,4,4096]{2,0,1:T(8,128)(2,1)} %bitcast.17), calls=%async_computation | async-start | bytes 1572864 | tf_op jit(solution)/shard_map/all_to_all | solution.py:25
  12.9 17.3 %copy-start = (s32[768,1]{0,1:T(1,128)S(1)}, s32[768,1]{0,1:T(1,128)}, u32[]{:S(2)}) copy-start(s32[768,1]{0,1:T(1,128)} %param.6) | copy-start | bytes 9220
  12.9 17.4 %copy-start.1 = (s32[768]{0:T(1024)S(1)}, s32[768]{0:T(1024)}, u32[]{:S(2)}) copy-start(s32[768]{0:T(1024)} %param.7) | copy-start | bytes 9220
  24.4 42.0 %all-to-all-start.1 = ((bf16[8,24,4096]{2,1,0:T(8,128)(2,1)}), bf16[8,24,4096]{2,1,0:T(8,128)(2,1)S(1)}, u32[]{:S(2)}, u32[]{:S(2)}) async-start(bf16[8,24,4096]{2,1,0:T(8,128)(2,1)} %bitcast.22), calls=%async_computation.1 | async-start | bytes 3145728 | tf_op jit(solution)/shard_map/all_to_all | solution.py:49
  30.1 141.7 %all-gather.2.cloned.1.call-start = ((), (), s32[]{:S(2)}) async-start(), calls=%async_computation.2 | async-start | bytes 7667712 | tf_op jit(solution)/shard_map/all_gather | solution.py:63
  67.6 180.7 %all-reduce.2.cloned.1.call-start = ((), (), s32[]{:S(2)}) async-start(), calls=%async_computation.3 | async-start | bytes 6815744 | tf_op jit(solution)/shard_map/psum | solution.py:11
  176.6 0.7 copy-start.2
  176.6 0.8 copy-start.3
Sparse Core Ops, SparseCore 0:
  67.8 104.0 all-gather.1
  176.7 71.5 all-reduce.1
where the time goes:
time: 283 us; the launch traced here: 280 us
  waiting for transfers between devices  210 us (74%)
  matrix products  27.4 us (10%)
  between operations  13.6 us (5%)
  local copies, waits for them, and re-layouts  12.1 us (4%)
  starting transfers between devices  10.1 us (4%)
  other arithmetic  6.84 us (2%)
    all_gather x1, waiting for transfers between devices, local(): gathered = lax.all_gather(panel, 'col', axis=0, tiled=True)  104 us
    psum x1, waiting for transfers between devices, from_root(): return lax.psum(kept, axis)  67.4 us
    all_to_all x1, waiting for transfers between devices, local(): lax.all_to_all(outgoing, 'col', split_axis=0, concat_axis=0, tiled=True)  32.6 us
    dot_general x1, matrix products, local(): lax.dot_general(gathered, scaled, (((0,), (0,)), ((), ())), preferred_ele...  25.3 us
    all_to_all x1, waiting for transfers between devices, local(): lax.all_to_all(jac, 'row', split_axis=1, concat_axis=0, tiled=True)  6.27 us
    all_to_all x1, starting transfers between devices, local(): lax.all_to_all(outgoing, 'col', split_axis=0, concat_axis=0, tiled=True)  5.77 us
  transfers between devices with their start and end apart: 4, of which 4 were waited for; matrix products, arithmetic and copies ran while one was open for 4% of the time, Pallas kernels for 0%

commit v1 on v0

v1 whole, which is shorter than its diff:
```python
import functools

import jax
import jax.numpy as jnp
from jax import lax
from jax.experimental import pallas as pl
from jax.experimental.pallas import tpu as pltpu
from jax.sharding import PartitionSpec as P

BPC = 8
MESH = pl.DeviceIdType.MESH


def gather_kernel(n_col, block, win, jac, a, w, loc, s1, ra, rw, sr, sl, sy, sw, sx, so):
    length = n_col // 2
    r, c = lax.axis_index("row"), lax.axis_index("col")
    z, y = c // 2, c % 2
    r1 = r + 1 - 2 * (r % 2)
    r2 = (r + 2) % 4
    r3 = (r1 + 2) % 4
    root = c // (block // win)
    root1 = root + 1 - 2 * (root % 2)
    root2 = (root + 2) % 4
    off = pl.multiple_of((c % (block // win)) * win, win)
    is_root, is_relay = r == root, r == root2
    has_right, has_left = z < length - 1, z > 0
    right, left, across = c + 2, c - 2, c + 1 - 2 * y

    barrier = pltpu.get_barrier_semaphore()

    def greet(row, col):
        pl.semaphore_signal(barrier, inc=1, device_id=(row, col), device_id_type=MESH)

    for peer in (r1, r2, r3):
        greet(peer, c)
    greet(r, across)

    @pl.when(has_right)
    def _():
        greet(r, right)

    @pl.when(has_left)
    def _():
        greet(r, left)

    pl.semaphore_wait(barrier, 4 + jnp.where(has_right, 1, 0) + jnp.where(has_left, 1, 0))

    def remote(src, dst, send, recv, row, col):
        return pltpu.make_async_remote_copy(
            src_ref=src, dst_ref=dst, send_sem=send, recv_sem=recv, device_id=(row, col), device_id_type=MESH
        )

    mine = c * 4 + r
    own = pltpu.make_async_copy(jac.at[:, pl.ds(pl.multiple_of(r * block, block), block)], a.at[mine], loc)
    own.start()
    first = [
        remote(jac.at[:, pl.ds(pl.multiple_of(peer * block, block), block)], a.at[mine], s1.at[i], ra.at[mine], peer, c)
        for i, peer in enumerate((r1, r2, r3))
    ]
    for copy in (first[1], first[2], first[0]):
        copy.start()

    def a_copy(s, sems, col):
        return remote(a.at[s], a.at[s], sems.at[s // 8 * 4 + s % 4], ra.at[s], r, col)

    def a_wait(s):
        a_copy(s, sy, across).wait_recv()

    def w_copy(s, sems, row):
        return remote(a.at[s, :, pl.ds(off, win)], w.at[s], sems.at[s], rw.at[s], row, c)

    def w_own(s):
        return pltpu.make_async_copy(a.at[s, :, pl.ds(off, win)], w.at[s], so.at[s])

    def w_relay(s):
        return remote(w.at[s], w.at[s], sw.at[s], rw.at[s], r1, c)

    def w_start(s):
        @pl.when(is_root)
        def _():
            w_copy(s, sx, root2).start()
            w_copy(s, sw, root1).start()
            w_own(s).start()

    def w_pass(s):
        @pl.when(is_relay)
        def _():
            w_relay(s).wait_recv()
            w_relay(s).start()

    def send_right(s):
        @pl.when(has_right)
        def _():
            a_copy(s, sr, right).start()

    def send_left(s):
        @pl.when(has_left)
        def _():
            a_copy(s, sl, left).start()

    def send_across(s):
        a_copy(s, sy, across).start()

    for j, k in enumerate((r, r1, r2, r3)):
        s = c * 4 + k
        if j == 0:
            own.wait()
        else:
            a_wait(s)
        send_right(s)
        send_left(s)
        send_across(s)
        w_start(s)

    def both(d, k, lane, act_left, act_right, first_too):
        @pl.when((d >= (0 if first_too else 1)) & (d < length) & (z - d >= 0))
        def _():
            act_left(((z - d) * 2 + lane) * 4 + k)

        @pl.when((d >= 1) & (d < length) & (z + d < length))
        def _():
            act_right(((z + d) * 2 + lane) * 4 + k)

    def step(t, carry):
        d, j = t // 4, t % 4
        k = jnp.where(j == 0, r, jnp.where(j == 1, r1, jnp.where(j == 2, r2, r3)))

        def from_left(s):
            a_wait(s)
            send_right(s)
            send_across(s)
            w_start(s)

        def from_right(s):
            a_wait(s)
            send_left(s)
            send_across(s)
            w_start(s)

        def from_across(s):
            a_wait(s)
            w_start(s)

        both(d, k, y, from_left, from_right, False)
        both(d - 1, k, 1 - y, from_across, from_across, True)
        both(d - 1, k, y, w_pass, w_pass, True)
        both(d - 2, k, 1 - y, w_pass, w_pass, True)
        return carry

    lax.fori_loop(4, (length + 2) * 4, step, 0)

    def finish(i, carry):
        zz, k = i // 4, i % 4
        s = (zz * 2 + y) * 4 + k
        a_copy(s, sy, across).wait_send()

        @pl.when(has_right & (zz <= z))
        def _():
            a_copy(s, sr, right).wait_send()

        @pl.when(has_left & (zz >= z))
        def _():
            a_copy(s, sl, left).wait_send()

        return carry

    lax.fori_loop(0, length * 4, finish, 0)

    def finish_w(s, carry):
        @pl.when(is_root)
        def _():
            w_copy(s, sx, root2).wait_send()
            w_copy(s, sw, root1).wait_send()
            w_own(s).wait()

        @pl.when(is_relay)
        def _():
            w_relay(s).wait_send()

        @pl.when(jnp.logical_not(is_root | is_relay))
        def _():
            w_relay(s).wait_recv()

        return carry

    lax.fori_loop(0, n_col * 4, finish_w, 0)
    for copy in first:
        copy.wait_send()


def product_kernel(g_col, g_row, diag, corr, a, w, out, scaled):
    points, win = w.shape
    nblocks = corr.shape[0]

    @pl.when(pl.program_id(0) == 0)
    def _():
        hit = g_col[...] == lax.broadcasted_iota(jnp.int32, (points, nblocks), 1)
        scale = jnp.sum(jnp.where(hit, diag[...], 0.0), axis=1, keepdims=True)
        spread = jnp.where(hit, 1.0, 0.0).astype(jnp.bfloat16)
        member = jnp.where(g_row[...] == lax.broadcasted_iota(jnp.int32, (nblocks, points), 0), 1.0, 0.0).astype(
            jnp.bfloat16
        )

        @pl.loop(0, win // 256)
        def _(i):
            cols = pl.ds(pl.multiple_of(i * 256, 256), 256)
            part = w[:, cols]
            sums = jnp.dot(member, part, preferred_element_type=jnp.float32).astype(jnp.bfloat16)
            rows = (corr[...] * sums.astype(jnp.float32)).astype(jnp.bfloat16)
            back = jnp.dot(spread, rows, preferred_element_type=jnp.float32)
            scaled[:, cols] = (scale * part.astype(jnp.float32) + back).astype(jnp.bfloat16)

    out[...] = lax.dot_general(
        a[...], scaled[...], (((0,), (0,)), ((), ())), preferred_element_type=jnp.float32
    )


def local(jac, owner_list, block_id, diag_weight, corr_weight):
    n_row, n_col = lax.axis_size("row"), lax.axis_size("col")
    pt_dev, width = jac.shape
    points = owner_list.shape[0]
    block, win = width // n_row, width // n_col
    slots = n_row * n_col
    nblocks = diag_weight.shape[0]
    dma = pltpu.SemaphoreType.DMA
    a, w = pl.pallas_call(
        functools.partial(gather_kernel, n_col, block, win),
        out_shape=(
            jax.ShapeDtypeStruct((slots, pt_dev, block), jac.dtype),
            jax.ShapeDtypeStruct((slots, pt_dev, win), jac.dtype),
        ),
        in_specs=[pl.BlockSpec(memory_space=pl.ANY)],
        out_specs=(pl.BlockSpec(memory_space=pl.ANY), pl.BlockSpec(memory_space=pl.ANY)),
        scratch_shapes=[
            dma(()), dma((3,)), dma((slots,)), dma((slots,)), dma((slots // 2,)), dma((slots // 2,)),
            dma((slots // 2,)), dma((slots,)), dma((slots,)), dma((slots,)),
        ],
        compiler_params=pltpu.CompilerParams(collective_id=0, has_side_effects=True),
        name="gather",
    )(jac)
    a = a.reshape(points, block)
    w = w.reshape(points, win)
    group = owner_list[:, 0] * BPC + block_id
    group = group.reshape(n_row, n_col, pt_dev).transpose(1, 0, 2).reshape(points)
    tile = 512
    whole = lambda *shape: pl.BlockSpec(shape, lambda i: (0, 0))
    return pl.pallas_call(
        product_kernel,
        grid=(block // tile,),
        out_shape=jax.ShapeDtypeStruct((block, win), jnp.float32),
        in_specs=[
            whole(points, 1), whole(1, points), whole(1, nblocks), whole(nblocks, 1),
            pl.BlockSpec((points, tile), lambda i: (0, i)), whole(points, win),
        ],
        out_specs=pl.BlockSpec((tile, win), lambda i: (i, 0)),
        scratch_shapes=[pltpu.VMEM((points, win), jnp.bfloat16)],
        compiler_params=pltpu.CompilerParams(vmem_limit_bytes=56 * 1024 * 1024),
        cost_estimate=pl.CostEstimate(flops=2 * points * block * win, bytes_accessed=4 * block * win, transcendentals=0),
        name="product",
    )(group[:, None], group[None, :], diag_weight[None, :], corr_weight[:, None], a, w)


def solution(mesh):
    in_specs = (P(("row", "col"), None), P(), P(), P(), P())
    out_specs = P("row", "col")
    return jax.shard_map(local, mesh=mesh, in_specs=in_specs, out_specs=out_specs, check_vma=False)
```

time: 283 us -> 137 us (0.48)
  the two profiles are of different devices: /device:TPU:7 before, /device:TPU:0 now
where the time goes in v1:
time: 137 us
  Pallas kernels  132 us (96%)
  local copies, waits for them, and re-layouts  3.04 us (2%)
  other arithmetic  1.39 us (1%)
    pallas_call x1, Pallas kernels, local(): pl.pallas_call(functools.partial(gather_kernel, n_col, block, win), out_s...  108 us
    pallas_call x1, Pallas kernels, local(): pl.pallas_call(product_kernel, grid=(block // tile,), out_shape=jax.Shape...  24.1 us

profile of v1, /device:TPU:0, one launch (start us, length us, event | category | flops | bytes accessed | tf_op | source)
XLA Modules:
  0.0 136.9 jit_solution(4998585868892922885)
XLA Ops:
  0.0 0.7 multiply_reduce_fusion
  0.7 0.7 add.3
  1.4 0.1 reshape.11
  1.5 0.7 broadcast_in_dim_reshape.7.g_row
  2.2 1.4 copy.10.corr
  3.5 0.9 broadcast_in_dim_reshape.8.g_col
  4.5 108.4 %gather.1 = (bf16[32,24,4096]{2,1,0:T(8,128)(2,1)}, bf16[32,24,2048]{2,1,0:T(8,128)(2,1)}) custom-call(bf16[24,16384]{1,0:T(8,128)(2,1)} %jac.1), custom_call_target="tpu_custom_call" | custom-call | tf_op jit(solution)/shard_map/gather/pallas_call | solution.py:226
  112.8 24.1 %product.1 = f32[4096,2048]{1,0:T(8,128)} custom-call(s32[768,1]{1,0:T(8,128)} %broadcast_in_dim_reshape.8.g_col, s32[1,768]{1,0:T(1,128)} %broadcast_in_dim_reshape.7.g_row, f32[1,64]{1,0:T(1,128)} %bitcast.9, f32[64,1]{1,0:T(8,128)} %copy.10.corr, bf16[768,4096]{1,0:T(8,128)(2,1)} %bitcast.7, bf16[768,2048]{1,0:T(8,128)(2,1)} %bitcast.8), custom_call_target="tpu_custom_call" | custom-call | flops 12884901888 | bytes 33554432 | tf_op jit(solution)/shard_map/product/pallas_call | solution.py:247
  (1 shorter events, 0.0 us)

commit v2 on v1

--- a/solution.py
+++ b/solution.py
@@ -11,7 +11,7 @@
 MESH = pl.DeviceIdType.MESH
 
 
-def gather_kernel(n_col, block, win, jac, a, w, loc, s1, ra, rw, sr, sl, sy, sw, sx, so):
+def gather_kernel(n_col, block, win, jac, a, w, loc, s1, ra, rw, sr, sl, sy, sw, sx):
     length = n_col // 2
     r, c = lax.axis_index("row"), lax.axis_index("col")
     z, y = c // 2, c % 2
@@ -50,7 +50,7 @@
             src_ref=src, dst_ref=dst, send_sem=send, recv_sem=recv, device_id=(row, col), device_id_type=MESH
         )
 
-    mine = c * 4 + r
+    mine = r * n_col + c
     own = pltpu.make_async_copy(jac.at[:, pl.ds(pl.multiple_of(r * block, block), block)], a.at[mine], loc)
     own.start()
     first = [
@@ -61,7 +61,7 @@
         copy.start()
 
     def a_copy(s, sems, col):
-        return remote(a.at[s], a.at[s], sems.at[s // 8 * 4 + s % 4], ra.at[s], r, col)
+        return remote(a.at[s], a.at[s], sems.at[s % n_col // 2 * 4 + s // n_col], ra.at[s], r, col)
 
     def a_wait(s):
         a_copy(s, sy, across).wait_recv()
@@ -69,9 +69,6 @@
     def w_copy(s, sems, row):
         return remote(a.at[s, :, pl.ds(off, win)], w.at[s], sems.at[s], rw.at[s], row, c)
 
-    def w_own(s):
-        return pltpu.make_async_copy(a.at[s, :, pl.ds(off, win)], w.at[s], so.at[s])
-
     def w_relay(s):
         return remote(w.at[s], w.at[s], sw.at[s], rw.at[s], r1, c)
 
@@ -80,7 +77,6 @@
         def _():
             w_copy(s, sx, root2).start()
             w_copy(s, sw, root1).start()
-            w_own(s).start()
 
     def w_pass(s):
         @pl.when(is_relay)
@@ -102,7 +98,7 @@
         a_copy(s, sy, across).start()
 
     for j, k in enumerate((r, r1, r2, r3)):
-        s = c * 4 + k
+        s = k * n_col + c
         if j == 0:
             own.wait()
         else:
@@ -115,11 +111,11 @@
     def both(d, k, lane, act_left, act_right, first_too):
         @pl.when((d >= (0 if first_too else 1)) & (d < length) & (z - d >= 0))
         def _():
-            act_left(((z - d) * 2 + lane) * 4 + k)
+            act_left(k * n_col + (z - d) * 2 + lane)
 
         @pl.when((d >= 1) & (d < length) & (z + d < length))
         def _():
-            act_right(((z + d) * 2 + lane) * 4 + k)
+            act_right(k * n_col + (z + d) * 2 + lane)
 
     def step(t, carry):
         d, j = t // 4, t % 4
@@ -151,7 +147,7 @@
 
     def finish(i, carry):
         zz, k = i // 4, i % 4
-        s = (zz * 2 + y) * 4 + k
+        s = k * n_col + zz * 2 + y
         a_copy(s, sy, across).wait_send()
 
         @pl.when(has_right & (zz <= z))
@@ -171,7 +167,6 @@
         def _():
             w_copy(s, sx, root2).wait_send()
             w_copy(s, sw, root1).wait_send()
-            w_own(s).wait()
 
         @pl.when(is_relay)
         def _():
@@ -188,25 +183,40 @@
         copy.wait_send()
 
 
-def product_kernel(g_col, g_row, diag, corr, a, w, out, scaled):
+def product_kernel(group, diag, corr, a, a_all, w_all, out, w, scaled, sem):
     points, win = w.shape
-    nblocks = corr.shape[0]
+    nblocks = corr.shape[1]
+    per_row = a_all.shape[1] // win
 
     @pl.when(pl.program_id(0) == 0)
     def _():
-        hit = g_col[...] == lax.broadcasted_iota(jnp.int32, (points, nblocks), 1)
-        scale = jnp.sum(jnp.where(hit, diag[...], 0.0), axis=1, keepdims=True)
-        spread = jnp.where(hit, 1.0, 0.0).astype(jnp.bfloat16)
-        member = jnp.where(g_row[...] == lax.broadcasted_iota(jnp.int32, (nblocks, points), 0), 1.0, 0.0).astype(
-            jnp.bfloat16
-        )
-
-        @pl.loop(0, win // 256)
-        def _(i):
-            cols = pl.ds(pl.multiple_of(i * 256, 256), 256)
+        r, c = lax.axis_index("row"), lax.axis_index("col")
+        off = pl.multiple_of((c % per_row) * win, win)
+        is_root = r == c // per_row
+
+        @pl.when(is_root)
+        def _():
+            pltpu.make_async_copy(a_all.at[:, pl.ds(off, win)], w, sem).start()
+
+        @pl.when(jnp.logical_not(is_root))
+        def _():
+            pltpu.make_async_copy(w_all, w, sem).start()
+
+        block = lax.broadcasted_iota(jnp.int32, (nblocks, points), 0)
+        member = jnp.where(group[...] == block, 1.0, 0.0)
+        spread = member.T
+        scale = jnp.sum(spread * diag[...], axis=1, keepdims=True)
+        member, spread = member.astype(jnp.bfloat16), spread.astype(jnp.bfloat16)
+        square = (nblocks, nblocks)
+        same = lax.broadcasted_iota(jnp.int32, square, 0) == lax.broadcasted_iota(jnp.int32, square, 1)
+        weight = jnp.sum(jnp.where(same, corr[...], 0.0), axis=1, keepdims=True)
+        pltpu.make_async_copy(w_all, w, sem).wait()
+        wide = min(win, 512)
+        for i in range(win // wide):
+            cols = slice(i * wide, (i + 1) * wide)
             part = w[:, cols]
             sums = jnp.dot(member, part, preferred_element_type=jnp.float32).astype(jnp.bfloat16)
-            rows = (corr[...] * sums.astype(jnp.float32)).astype(jnp.bfloat16)
+            rows = (weight * sums.astype(jnp.float32)).astype(jnp.bfloat16)
             back = jnp.dot(spread, rows, preferred_element_type=jnp.float32)
             scaled[:, cols] = (scale * part.astype(jnp.float32) + back).astype(jnp.bfloat16)
 
@@ -233,15 +243,14 @@
         out_specs=(pl.BlockSpec(memory_space=pl.ANY), pl.BlockSpec(memory_space=pl.ANY)),
         scratch_shapes=[
             dma(()), dma((3,)), dma((slots,)), dma((slots,)), dma((slots // 2,)), dma((slots // 2,)),
-            dma((slots // 2,)), dma((slots,)), dma((slots,)), dma((slots,)),
+            dma((slots // 2,)), dma((slots,)), dma((slots,)),
         ],
         compiler_params=pltpu.CompilerParams(collective_id=0, has_side_effects=True),
         name="gather",
     )(jac)
     a = a.reshape(points, block)
     w = w.reshape(points, win)
-    group = owner_list[:, 0] * BPC + block_id
-    group = group.reshape(n_row, n_col, pt_dev).transpose(1, 0, 2).reshape(points)
+    group = owner_list.reshape(1, points) * BPC + block_id.reshape(1, points)
     tile = 512
     whole = lambda *shape: pl.BlockSpec(shape, lambda i: (0, 0))
     return pl.pallas_call(
@@ -249,15 +258,16 @@
         grid=(block // tile,),
         out_shape=jax.ShapeDtypeStruct((block, win), jnp.float32),
         in_specs=[
-            whole(points, 1), whole(1, points), whole(1, nblocks), whole(nblocks, 1),
-            pl.BlockSpec((points, tile), lambda i: (0, i)), whole(points, win),
+            whole(1, points), whole(1, nblocks), whole(1, nblocks),
+            pl.BlockSpec((points, tile), lambda i: (0, i)),
+            pl.BlockSpec(memory_space=pl.ANY), pl.BlockSpec(memory_space=pl.ANY),
         ],
         out_specs=pl.BlockSpec((tile, win), lambda i: (i, 0)),
-        scratch_shapes=[pltpu.VMEM((points, win), jnp.bfloat16)],
+        scratch_shapes=[pltpu.VMEM((points, win), jnp.bfloat16)] * 2 + [dma(())],
         compiler_params=pltpu.CompilerParams(vmem_limit_bytes=56 * 1024 * 1024),
         cost_estimate=pl.CostEstimate(flops=2 * points * block * win, bytes_accessed=4 * block * win, transcendentals=0),
         name="product",
-    )(group[:, None], group[None, :], diag_weight[None, :], corr_weight[:, None], a, w)
+    )(group, diag_weight[None, :], corr_weight[None, :], a, a, w)
 
 
 def solution(mesh):

time: 137 us -> 111 us (0.81)
  the two profiles are of different devices: /device:TPU:0 before, /device:TPU:7 now
where the time goes in v2:
time: 111 us; the launch traced here: 109 us
  Pallas kernels  107 us (96%)
  other arithmetic  1.39 us (1%)
    pallas_call x1, Pallas kernels, local(): pl.pallas_call(functools.partial(gather_kernel, n_col, block, win), out_s...  85 us
    pallas_call x1, Pallas kernels, local(): pl.pallas_call(product_kernel, grid=(block // tile,), out_shape=jax.Shape...  22.3 us

profile of v2, /device:TPU:7, one launch (start us, length us, event | category | flops | bytes accessed | tf_op | source)
XLA Modules:
  0.0 109.3 jit_solution(4142387469642548615)
XLA Ops:
  0.0 0.7 multiply_reduce_fusion
  0.7 0.7 add.5
  1.4 0.6 add.6.group
  2.0 85.0 %gather.1 = (bf16[32,24,4096]{2,1,0:T(8,128)(2,1)}, bf16[32,24,2048]{2,1,0:T(8,128)(2,1)}) custom-call(bf16[24,16384]{1,0:T(8,128)(2,1)} %jac.1), custom_call_target="tpu_custom_call" | custom-call | tf_op jit(solution)/shard_map/gather/pallas_call | solution.py:236
  87.0 22.3 %product.1 = f32[4096,2048]{1,0:T(8,128)} custom-call(s32[1,768]{1,0:T(1,128)} %add.6.group, f32[1,64]{1,0:T(1,128)} %bitcast.7, f32[1,64]{1,0:T(1,128)} %bitcast.8, bf16[768,4096]{1,0:T(8,128)(2,1)} %bitcast.4, bf16[768,4096]{1,0:T(8,128)(2,1)} %bitcast.5, bf16[768,2048]{1,0:T(8,128)(2,1)} %bitcast.6), custom_call_target="tpu_custom_call" | custom-call | flops 12884901888 | bytes 33554432 | tf_op jit(solution)/shard_map/product/pallas_call | solution.py:256

commit v3 on v2

--- a/solution.py
+++ b/solution.py
@@ -11,7 +11,7 @@
 MESH = pl.DeviceIdType.MESH
 
 
-def gather_kernel(n_col, block, win, jac, a, w, loc, s1, ra, rw, sr, sl, sy, sw, sx):
+def gather_kernel(n_col, block, win, jac, a, w, loc, s1, sn, rn, rb, rw, nr, nl, sr, sl, sy, sw, sx):
     length = n_col // 2
     r, c = lax.axis_index("row"), lax.axis_index("col")
     z, y = c // 2, c % 2
@@ -54,14 +54,31 @@
     own = pltpu.make_async_copy(jac.at[:, pl.ds(pl.multiple_of(r * block, block), block)], a.at[mine], loc)
     own.start()
     first = [
-        remote(jac.at[:, pl.ds(pl.multiple_of(peer * block, block), block)], a.at[mine], s1.at[i], ra.at[mine], peer, c)
+        remote(jac.at[:, pl.ds(pl.multiple_of(peer * block, block), block)], a.at[mine], s1.at[i], rb.at[mine], peer, c)
         for i, peer in enumerate((r1, r2, r3))
     ]
     for copy in (first[1], first[2], first[0]):
         copy.start()
 
+    cut = block * 5 // 32
+    near, far = pl.ds(0, cut), pl.ds(cut, block - cut)
+
+    def n_copy(s, send, col):
+        return remote(a.at[s, :, near], a.at[s, :, near], send, rn.at[s], r, col)
+
+    def n_across(s):
+        return n_copy(s, sn.at[s // n_col], across)
+
+    def n_right(s):
+        return n_copy(s, nr.at[s], right)
+
+    def n_left(s):
+        return n_copy(s, nl.at[s], left)
+
     def a_copy(s, sems, col):
-        return remote(a.at[s], a.at[s], sems.at[s % n_col // 2 * 4 + s // n_col], ra.at[s], r, col)
+        return remote(
+            a.at[s, :, far], a.at[s, :, far], sems.at[s % n_col // 2 * 4 + s // n_col], rb.at[s], r, col
+        )
 
     def a_wait(s):
         a_copy(s, sy, across).wait_recv()
@@ -93,6 +110,16 @@
         @pl.when(has_left)
         def _():
             a_copy(s, sl, left).start()
+
+    def near_right(s):
+        @pl.when(has_right)
+        def _():
+            n_right(s).start()
+
+    def near_left(s):
+        @pl.when(has_left)
+        def _():
+            n_left(s).start()
 
     def send_across(s):
         a_copy(s, sy, across).start()
@@ -102,10 +129,13 @@
         if j == 0:
             own.wait()
         else:
-            a_wait(s)
+            remote(a.at[s], a.at[s], s1.at[0], rb.at[s], r1, c).wait_recv()
+        n_across(s).start()
         send_right(s)
         send_left(s)
         send_across(s)
+        near_right(s)
+        near_left(s)
         w_start(s)
 
     def both(d, k, lane, act_left, act_right, first_too):
@@ -125,19 +155,36 @@
             a_wait(s)
             send_right(s)
             send_across(s)
+            n_across(s).wait_recv()
+            near_right(s)
             w_start(s)
 
         def from_right(s):
             a_wait(s)
             send_left(s)
             send_across(s)
+            n_across(s).wait_recv()
+            near_left(s)
             w_start(s)
+
+        def near_from_left(s):
+            n_across(s).wait_recv()
+            near_right(s)
+
+            @pl.when(d == 1)
+            def _():
+                near_left(s)
+
+        def near_from_right(s):
+            n_across(s).wait_recv()
+            near_left(s)
 
         def from_across(s):
             a_wait(s)
             w_start(s)
 
         both(d, k, y, from_left, from_right, False)
+        both(d - 1, k, 1 - y, near_from_left, near_from_right, True)
         both(d - 1, k, 1 - y, from_across, from_across, True)
         both(d - 1, k, y, w_pass, w_pass, True)
         both(d - 2, k, 1 - y, w_pass, w_pass, True)
@@ -162,7 +209,20 @@
 
     lax.fori_loop(0, length * 4, finish, 0)
 
+    for k in range(4):
+        n_across(k * n_col + c).wait_send()
+
     def finish_w(s, carry):
+        zz = s % n_col // 2
+
+        @pl.when(has_right & (zz <= z))
+        def _():
+            n_right(s).wait_send()
+
+        @pl.when(has_left & (zz >= z))
+        def _():
+            n_left(s).wait_send()
+
         @pl.when(is_root)
         def _():
             w_copy(s, sx, root2).wait_send()
@@ -242,8 +302,8 @@
         in_specs=[pl.BlockSpec(memory_space=pl.ANY)],
         out_specs=(pl.BlockSpec(memory_space=pl.ANY), pl.BlockSpec(memory_space=pl.ANY)),
         scratch_shapes=[
-            dma(()), dma((3,)), dma((slots,)), dma((slots,)), dma((slots // 2,)), dma((slots // 2,)),
-            dma((slots // 2,)), dma((slots,)), dma((slots,)),
+            dma(()), dma((3,)), dma((n_row,)), dma((slots,)), dma((slots,)), dma((slots,)), dma((slots,)), dma((slots,)),
+            dma((slots // 2,)), dma((slots // 2,)), dma((slots // 2,)), dma((slots,)), dma((slots,)),
         ],
         compiler_params=pltpu.CompilerParams(collective_id=0, has_side_effects=True),
         name="gather",

time: 111 us -> 105 us (0.946); the launches traced: 109 us -> 105 us
  Pallas kernels: 107 us -> 103 us
    pallas_call x1, Pallas kernels: 85 us -> 80.8 us  [local(): pl.pallas_call(functools.partial(gather_kernel, n_col, block, win), out_s...]
where the time goes in v3:
time: 105 us
  Pallas kernels  103 us (98%)
  other arithmetic  1.39 us (1%)
    pallas_call x1, Pallas kernels, local(): pl.pallas_call(functools.partial(gather_kernel, n_col, block, win), out_s...  80.8 us
    pallas_call x1, Pallas kernels, local(): pl.pallas_call(product_kernel, grid=(block // tile,), out_shape=jax.Shape...  22.3 us

profile of v3, /device:TPU:7, one launch (start us, length us, event | category | flops | bytes accessed | tf_op | source)
XLA Modules:
  0.0 105.1 jit_solution(15992678829743208866)
XLA Ops:
  0.0 0.7 multiply_reduce_fusion
  0.7 0.7 add.5
  1.4 0.6 add.6.group
  2.0 80.8 %gather.1 = (bf16[32,24,4096]{2,1,0:T(8,128)(2,1)}, bf16[32,24,2048]{2,1,0:T(8,128)(2,1)}) custom-call(bf16[24,16384]{1,0:T(8,128)(2,1)} %jac.1), custom_call_target="tpu_custom_call" | custom-call | tf_op jit(solution)/shard_map/gather/pallas_call | solution.py:296
  82.8 22.3 %product.1 = f32[4096,2048]{1,0:T(8,128)} custom-call(s32[1,768]{1,0:T(1,128)} %add.6.group, f32[1,64]{1,0:T(1,128)} %bitcast.7, f32[1,64]{1,0:T(1,128)} %bitcast.8, bf16[768,4096]{1,0:T(8,128)(2,1)} %bitcast.4, bf16[768,4096]{1,0:T(8,128)(2,1)} %bitcast.5, bf16[768,2048]{1,0:T(8,128)(2,1)} %bitcast.6), custom_call_target="tpu_custom_call" | custom-call | flops 12884901888 | bytes 33554432 | tf_op jit(solution)/shard_map/product/pallas_call | solution.py:316

commit v4 on v3

--- a/solution.py
+++ b/solution.py
@@ -243,7 +243,7 @@
         copy.wait_send()
 
 
-def product_kernel(group, diag, corr, a, a_all, w_all, out, w, scaled, sem):
+def product_kernel(group, diag, corr, a, a_all, w_all, out, w, scaled, sem, held, sent):
     points, win = w.shape
     nblocks = corr.shape[1]
     per_row = a_all.shape[1] // win
@@ -280,9 +280,33 @@
             back = jnp.dot(spread, rows, preferred_element_type=jnp.float32)
             scaled[:, cols] = (scale * part.astype(jnp.float32) + back).astype(jnp.bfloat16)
 
-    out[...] = lax.dot_general(
-        a[...], scaled[...], (((0,), (0,)), ((), ())), preferred_element_type=jnp.float32
-    )
+    step, steps = pl.program_id(0), pl.num_programs(0)
+    tile = a.shape[1]
+    slot = step % 2
+    wide = min(win, 512)
+
+    def store(at, i):
+        cols = pl.ds(i * wide, wide)
+        rows = pl.ds(pl.multiple_of(at * tile, tile), tile)
+        return pltpu.make_async_copy(held.at[at % 2, :, cols], out.at[rows, cols], sent.at[at % 2, i])
+
+    for i in range(win // wide):
+
+        @pl.when(step >= 2)
+        def _():
+            store(step - 2, i).wait()
+
+        cols = slice(i * wide, (i + 1) * wide)
+        held[slot, :, cols] = lax.dot_general(
+            a[...], scaled[:, cols], (((0,), (0,)), ((), ())), preferred_element_type=jnp.float32
+        )
+        store(step, i).start()
+
+    @pl.when(step == steps - 1)
+    def _():
+        for i in range(win // wide):
+            store(step - 1, i).wait()
+            store(step, i).wait()
 
 
 def local(jac, owner_list, block_id, diag_weight, corr_weight):
@@ -322,8 +346,9 @@
             pl.BlockSpec((points, tile), lambda i: (0, i)),
             pl.BlockSpec(memory_space=pl.ANY), pl.BlockSpec(memory_space=pl.ANY),
         ],
-        out_specs=pl.BlockSpec((tile, win), lambda i: (i, 0)),
-        scratch_shapes=[pltpu.VMEM((points, win), jnp.bfloat16)] * 2 + [dma(())],
+        out_specs=pl.BlockSpec(memory_space=pl.ANY),
+        scratch_shapes=[pltpu.VMEM((points, win), jnp.bfloat16)] * 2
+        + [dma(()), pltpu.VMEM((2, tile, win), jnp.float32), dma((2, max(1, win // 512)))],
         compiler_params=pltpu.CompilerParams(vmem_limit_bytes=56 * 1024 * 1024),
         cost_estimate=pl.CostEstimate(flops=2 * points * block * win, bytes_accessed=4 * block * win, transcendentals=0),
         name="product",

time: 105 us -> 109 us (1.038)
  Pallas kernels: 103 us -> 107 us
    pallas_call x1, Pallas kernels: 22.3 us -> 25.7 us  [local(): pl.pallas_call(product_kernel, grid=(block // tile,), out_shape=jax.Shape...]
where the time goes in v4:
time: 109 us
  Pallas kernels  107 us (98%)
  other arithmetic  1.39 us (1%)
    pallas_call x1, Pallas kernels, local(): pl.pallas_call(functools.partial(gather_kernel, n_col, block, win), out_s...  80.8 us
    pallas_call x1, Pallas kernels, local(): pl.pallas_call(product_kernel, grid=(block // tile,), out_shape=jax.Shape...  25.7 us

profile of v4, /device:TPU:7, one launch (start us, length us, event | category | flops | bytes accessed | tf_op | source)
XLA Modules:
  0.0 108.5 jit_solution(2162786472039185097)
XLA Ops:
  0.0 0.7 multiply_reduce_fusion
  0.7 0.7 add.5
  1.4 0.6 add.6.group
  2.0 80.8 %gather.1 = (bf16[32,24,4096]{2,1,0:T(8,128)(2,1)}, bf16[32,24,2048]{2,1,0:T(8,128)(2,1)}) custom-call(bf16[24,16384]{1,0:T(8,128)(2,1)} %jac.1), custom_call_target="tpu_custom_call" | custom-call | tf_op jit(solution)/shard_map/gather/pallas_call | solution.py:320
  82.8 25.7 %product.1 = f32[4096,2048]{1,0:T(8,128)} custom-call(s32[1,768]{1,0:T(1,128)} %add.6.group, f32[1,64]{1,0:T(1,128)} %bitcast.7, f32[1,64]{1,0:T(1,128)} %bitcast.8, bf16[768,4096]{1,0:T(8,128)(2,1)} %bitcast.4, bf16[768,4096]{1,0:T(8,128)(2,1)} %bitcast.5, bf16[768,2048]{1,0:T(8,128)(2,1)} %bitcast.6), custom_call_target="tpu_custom_call" | custom-call | flops 12884901888 | bytes 33554432 | tf_op jit(solution)/shard_map/product/pallas_call | solution.py:340

commit v5 on v3

--- a/solution.py
+++ b/solution.py
@@ -243,7 +243,7 @@
         copy.wait_send()
 
 
-def product_kernel(group, diag, corr, a, a_all, w_all, out, w, scaled, sem):
+def product_kernel(owner, ident, diag, corr, a, a_all, w_all, out, w, scaled, sem):
     points, win = w.shape
     nblocks = corr.shape[1]
     per_row = a_all.shape[1] // win
@@ -263,7 +263,7 @@
             pltpu.make_async_copy(w_all, w, sem).start()
 
         block = lax.broadcasted_iota(jnp.int32, (nblocks, points), 0)
-        member = jnp.where(group[...] == block, 1.0, 0.0)
+        member = jnp.where(owner[...] * BPC + ident[...] == block, 1.0, 0.0)
         spread = member.T
         scale = jnp.sum(spread * diag[...], axis=1, keepdims=True)
         member, spread = member.astype(jnp.bfloat16), spread.astype(jnp.bfloat16)
@@ -310,7 +310,6 @@
     )(jac)
     a = a.reshape(points, block)
     w = w.reshape(points, win)
-    group = owner_list.reshape(1, points) * BPC + block_id.reshape(1, points)
     tile = 512
     whole = lambda *shape: pl.BlockSpec(shape, lambda i: (0, 0))
     return pl.pallas_call(
@@ -318,7 +317,7 @@
         grid=(block // tile,),
         out_shape=jax.ShapeDtypeStruct((block, win), jnp.float32),
         in_specs=[
-            whole(1, points), whole(1, nblocks), whole(1, nblocks),
+            whole(1, points), whole(1, points), whole(1, nblocks), whole(1, nblocks),
             pl.BlockSpec((points, tile), lambda i: (0, i)),
             pl.BlockSpec(memory_space=pl.ANY), pl.BlockSpec(memory_space=pl.ANY),
         ],
@@ -327,7 +326,7 @@
         compiler_params=pltpu.CompilerParams(vmem_limit_bytes=56 * 1024 * 1024),
         cost_estimate=pl.CostEstimate(flops=2 * points * block * win, bytes_accessed=4 * block * win, transcendentals=0),
         name="product",
-    )(group, diag_weight[None, :], corr_weight[None, :], a, a, w)
+    )(owner_list.reshape(1, points), block_id.reshape(1, points), diag_weight[None, :], corr_weight[None, :], a, a, w)
 
 
 def solution(mesh):

time: 105 us -> 105 us (level)
  other arithmetic: 1.39 us -> 0 us
    reshape x0 -> x1, local copies, waits for them, and re-layouts: none -> 1.27 us  [local(): block_id.reshape(1, points)]
where the time goes in v5:
time: 105 us; the launch traced here: 104 us
  Pallas kernels  103 us (98%)
  local copies, waits for them, and re-layouts  1.27 us (1%)
    pallas_call x1, Pallas kernels, local(): pl.pallas_call(functools.partial(gather_kernel, n_col, block, win), out_s...  80.8 us
    pallas_call x1, Pallas kernels, local(): pl.pallas_call(product_kernel, grid=(block // tile,), out_shape=jax.Shape...  22.3 us

profile of v5, /device:TPU:7, one launch (start us, length us, event | category | flops | bytes accessed | tf_op | source)
XLA Modules:
  0.0 104.4 jit_solution(5465618560155761607)
XLA Ops:
  0.0 1.3 %reshape.13.ident = s32[1,768]{1,0:T(1,128)} reshape(s32[768]{0:T(1024)} %param.7) | data formatting | bytes 6144 | tf_op jit(solution)/shard_map/reshape | solution.py:329
  1.3 80.8 %gather.1 = (bf16[32,24,4096]{2,1,0:T(8,128)(2,1)}, bf16[32,24,2048]{2,1,0:T(8,128)(2,1)}) custom-call(bf16[24,16384]{1,0:T(8,128)(2,1)} %jac.1), custom_call_target="tpu_custom_call" | custom-call | tf_op jit(solution)/shard_map/gather/pallas_call | solution.py:296
  82.1 22.3 %product.1 = f32[4096,2048]{1,0:T(8,128)} custom-call(s32[1,768]{1,0:T(1,128)} %bitcast.8, s32[1,768]{1,0:T(1,128)} %reshape.13.ident, f32[1,64]{1,0:T(1,128)} %bitcast.9, f32[1,64]{1,0:T(1,128)} %bitcast.10, bf16[768,4096]{1,0:T(8,128)(2,1)} %bitcast.5, bf16[768,4096]{1,0:T(8,128)(2,1)} %bitcast.6, bf16[768,2048]{1,0:T(8,128)(2,1)} %bitcast.7), custom_call_target="tpu_custom_call" | custom-call | flops 12884901888 | bytes 33554432 | tf_op jit(solution)/shard_map/product/pallas_call | solution.py:315
